TPU v7x, 32 devices: a whole 2x2x4 slice. The times are simulated.
32 devices in a mesh: narrow: 2 (over core), wide: 16 (over z, y, x).
Axes of the slice: x: 2, y: 2, z: 4, core: 2. Of those that a mesh axis runs over, the one named last changes fastest.
Arguments:
- rows: bfloat16 [98304, 1024], P(('narrow', 'wide')), may hold values from -20 to 20
- list_ids: int32 [98304], P(('narrow', 'wide')), may hold values from 0 to 16383, as said below
- codes: int32 [98304, 64], P(('narrow', 'wide')), may hold values from 0 to 255
- row_counts: int32 [32], P(('narrow', 'wide')), may hold values from 1536 to 3072, as said below
- centroids: bfloat16 [16384, 1024], P('wide'), may hold values from -4 to 4
- old_codebook: float32 [64, 4096], replicated, may hold values from -4 to 4
Outputs:
- codebook: float32 [64, 4096], replicated
- search_table: bfloat16 [64, 4096], P('wide')
- row_error: float32 [98304], P(('narrow', 'wide'))
Inputs may be any that keep to these rules, and one draw needn't show every extreme that they name: `list_ids`: among the live passages of one device, at most 384 have lists owned by any one index w of wide (lists w * 1024 to (w + 1) * 1024 - 1), and one index of wide receives exactly 384 live passages from every device. Entries past a device's count are arbitrary. `row_counts`: one device holds exactly 3072 live passages.
All inputs are finite; a program needn't handle non-finite values.
Results may differ from a plain program's by a relative error of at most 0.00165.
Values may be sent and summed in bfloat16 or wider, within the bound.
A program may use at most 192 MiB of HBM per device.

v0:
```python
import math

import jax
import jax.numpy as jnp
from jax import lax
from jax.sharding import PartitionSpec as P

K = 256


def onehot_block(piece_codes, piece_valid, words):
    match = piece_codes[:, :, None] == jnp.arange(words, dtype=jnp.int32)[None, None, :]
    return (match & piece_valid[:, None, None]).astype(jnp.bfloat16)


def gram_sums(resid, codes, valid, words):
    total_rows, width_d = resid.shape
    spaces = codes.shape[1]
    sub_width = width_d // spaces
    block_rows = math.gcd(total_rows, 512)
    groups = total_rows // block_rows

    def absorb(carry, pieces):
        piece_rows, piece_codes, piece_valid = pieces
        onehot = onehot_block(piece_codes, piece_valid, words)
        shaped = piece_rows.reshape(block_rows, spaces, sub_width)
        sums = carry[0] + jnp.einsum(
            "bmk,bms->mks", onehot, shaped, preferred_element_type=jnp.float32
        )
        counts = carry[1] + jnp.sum(onehot, axis=0, dtype=jnp.float32)
        return ((sums, counts), None)

    start = (
        jnp.zeros((spaces, words, sub_width), jnp.float32),
        jnp.zeros((spaces, words), jnp.float32),
    )
    pieces = (
        resid.reshape(groups, block_rows, width_d),
        codes.reshape(groups, block_rows, spaces),
        valid.reshape(groups, block_rows),
    )
    (sums, counts), unused = lax.scan(absorb, start, pieces)
    return (sums.reshape(spaces, words * sub_width), counts)


def row_errors(resid, codes, valid, table):
    total_rows, width_d = resid.shape
    spaces, words, sub_width = table.shape
    block_rows = math.gcd(total_rows, 512)
    groups = total_rows // block_rows

    def measure(carry, pieces):
        piece_rows, piece_codes, piece_valid = pieces
        onehot = onehot_block(piece_codes, piece_valid, words)
        decoded = jnp.einsum("bmk,mks->bms", onehot, table, preferred_element_type=jnp.float32)
        diff = piece_rows.reshape(block_rows, spaces, sub_width).astype(jnp.float32) - decoded
        err = jnp.mean(diff * diff, axis=(1, 2))
        return (carry, jnp.where(piece_valid, err, jnp.float32(0.0)))

    pieces = (
        resid.reshape(groups, block_rows, width_d),
        codes.reshape(groups, block_rows, spaces),
        valid.reshape(groups, block_rows),
    )
    unused, errs = lax.scan(measure, jnp.float32(0.0), pieces)
    return errs.reshape(total_rows)


def refit(sums, counts, previous, anchor, words):
    spaces = sums.shape[0]
    sub_width = sums.shape[1] // words
    shaped = sums.reshape(spaces, words, sub_width) + anchor * previous.reshape(
        spaces, words, sub_width
    )
    return (shaped / (counts[:, :, None] + anchor)).reshape(spaces, words * sub_width)


def body(rows, list_ids, codes, row_counts, centroids, old_codebook):
    local_rows, width_d = rows.shape
    spaces = codes.shape[1]
    words = K
    sub_width = width_d // spaces
    wide_count = lax.axis_size("wide")
    capacity = 2 * local_rows // wide_count
    slots = wide_count * capacity
    lists_owned = centroids.shape[0]
    own_index = lax.axis_index("wide")
    anchor = float(local_rows * lax.axis_size("narrow") * wide_count // (4 * words))
    position = jnp.arange(local_rows, dtype=jnp.int32)
    is_live = position < row_counts[0]
    owner_index = jnp.where(is_live, list_ids // lists_owned, wide_count)
    member = (owner_index[:, None] == jnp.arange(wide_count, dtype=jnp.int32)[None, :]).astype(
        jnp.int32
    )
    ahead = jnp.cumsum(member, axis=0) - member
    within = jnp.sum(ahead * member, axis=1)
    slot_of_row = jnp.where(is_live, owner_index * capacity + within, slots)
    source_row = jnp.full((slots + 1,), local_rows, jnp.int32).at[slot_of_row].set(position)[:slots]
    padded_lists = jnp.concatenate([list_ids, jnp.full((1,), -1, jnp.int32)])
    send_lists = padded_lists[source_row].reshape(wide_count, capacity)
    asked = lax.all_to_all(send_lists, "wide", split_axis=0, concat_axis=0, tiled=True)
    wanted = jnp.clip(asked - own_index * lists_owned, 0, lists_owned - 1)
    found = jnp.where((asked >= 0)[:, :, None], centroids[wanted], jnp.zeros((), jnp.bfloat16))
    fetched = lax.all_to_all(found, "wide", split_axis=0, concat_axis=0, tiled=True)
    padded_fetch = jnp.concatenate(
        [fetched.reshape(slots, width_d), jnp.zeros((1, width_d), jnp.bfloat16)]
    )
    resid = (rows.astype(jnp.float32) - padded_fetch[slot_of_row].astype(jnp.float32)).astype(
        jnp.bfloat16
    )
    sums, counts = gram_sums(resid, codes, is_live, words)
    share = spaces // wide_count
    sums, counts = lax.psum((sums, counts), ("narrow", "wide"))
    codebook = refit(sums, counts, old_codebook, anchor, words)
    table_flat = codebook.astype(jnp.bfloat16)
    search_table = lax.dynamic_slice_in_dim(table_flat, own_index * share, share, 0)
    errs = row_errors(resid, codes, is_live, table_flat.reshape(spaces, words, sub_width))
    return (codebook, search_table, errs)


def solution(mesh):
    in_specs = (
        P(("narrow", "wide"), None),
        P(("narrow", "wide")),
        P(("narrow", "wide"), None),
        P(("narrow", "wide")),
        P("wide", None),
        P(),
    )
    out_specs = (P(), P("wide", None), P(("narrow", "wide")))
    return jax.shard_map(body, mesh=mesh, in_specs=in_specs, out_specs=out_specs, check_vma=False)
```

profile of v0, /device:TPU:0, one launch (start us, length us, event | category | flops | bytes accessed | tf_op | source)
XLA Modules:
  0.0 823.5 jit_solution(17916491600508764308)
XLA Ops:
  8.7 4.6 reduce-window.6
  15.6 11.8 %scatter_custom_fusion = s32[6145]{0:T(1024)S(1)} fusion(s32[3072]{0:T(1024)S(1)} %get-tuple-element.178, s32[3072]{0:T(1024)S(1)} %iota.40, s32[]{:T(128)} %constant.41.clone.1), kind=kCustom, calls=%fused_computation.54 | custom fusion | bytes 24584 | tf_op jit(solution)/shard_map/scatter | solution.py:98
  28.2 60.6 %gather_fusion = s32[6144]{0:T(1024)} fusion(s32[3073]{0:T(1024)S(1)} %pad_add_fusion, s32[6144]{0:T(1024)S(1)} %fusion.22), kind=kCustom, calls=%fused_computation | custom fusion | bytes 73728 | tf_op jit(solution)/shard_map/gather | solution.py:100
  88.7 8.3 %all-to-all-start = ((s32[16,1,384]{2,1,0:T(1,128)}), s32[16,1,384]{2,1,0:T(1,128)S(1)}, u32[]{:S(2)}, u32[]{:S(2)}) async-start(s32[16,1,384]{2,1,0:T(1,128)} %bitcast.7), calls=%async_computation | async-start | bytes 49152 | tf_op jit(solution)/shard_map/all_to_all | solution.py:101
  97.1 7.4 all-to-all-done
  104.5 26.8 %gather_fusion.1 = bf16[6144,1024]{1,0:T(8,128)(2,1)} fusion(bf16[1024,1024]{1,0:T(8,128)(2,1)S(1)} %copy-done, s32[6144]{0:T(1024)S(1)} %broadcast_clamp_fusion), kind=kCustom, calls=%fused_computation.1 | custom fusion | bytes 25190400 | tf_op jit(solution)/shard_map/gather | solution.py:103
  131.3 10.7 %broadcast_select_fusion = bf16[16,384,1024]{2,1,0:T(8,128)(2,1)} fusion(bf16[16,384,1024]{2,1,0:T(8,128)(2,1)} %bitcast.72, pred[16,384]{1,0:T(8,128)(4,1)S(1)} %compare_bitcast_fusion), kind=kLoop, calls=%fused_computation.30 | loop fusion | flops 6291456 | bytes 25171968 | tf_op jit(solution)/shard_map/jit(_where)/select_n | solution.py:103
  142.1 5.1 all-to-all-start.1
  147.3 233.6 %all-to-all-done.1 = bf16[16,384,1024]{2,1,0:T(8,128)(2,1)} async-done(((bf16[16,384,1024]{2,1,0:T(8,128)(2,1)}), bf16[16,384,1024]{2,1,0:T(8,128)(2,1)}, u32[]{:S(2)}, u32[]{:S(2)}) %all-to-all-start.1) | async-done | bytes 12582944 | tf_op jit(solution)/shard_map/all_to_all | solution.py:104
  380.9 10.5 %concatenate.7 = bf16[6145,1024]{1,0:T(8,128)(2,1)} pad(bf16[6144,1024]{1,0:T(8,128)(2,1)} %bitcast.11, bf16[]{:T(256)} %constant.84.clone.1), padding=0_1x0_0 | pad | bytes 25167874 | tf_op jit(solution)/shard_map/concatenate | solution.py:105
  391.4 22.2 %gather_fusion.2 = bf16[3072,1024]{1,0:T(8,128)(2,1)} fusion(bf16[6145,1024]{1,0:T(8,128)(2,1)} %concatenate.7, s32[3072]{0:T(1024)S(1)} %get-tuple-element.177), kind=kCustom, calls=%fused_computation.2 | custom fusion | bytes 12595200 | tf_op jit(solution)/shard_map/gather | solution.py:108
  413.6 10.5 %subtract_convert_fusion = bf16[3072,1024]{1,0:T(8,128)(2,1)} fusion(bf16[3072,1024]{1,0:T(8,128)(2,1)} %gather_fusion.2, bf16[3072,1024]{1,0:T(8,128)(2,1)} %param.10), kind=kLoop, calls=%fused_computation.29 | loop fusion | flops 12582912 | bytes 18874368 | tf_op jit(solution)/shard_map/convert_element_type | solution.py:108
  424.0 8.7 %copy.36 = bf16[6,512,1024]{1,2,0:T(8,128)(2,1)} copy(bf16[6,512,1024]{2,1,0:T(8,128)(2,1)} %bitcast.75) | data formatting | bytes 12582912
  432.7 122.1 %while.24 = (s32[]{:T(128)}, f32[64,256,16]{1,2,0:T(8,128)}, f32[64,256]{1,0:T(8,128)S(1)}, s32[6,512,64]{1,2,0:T(8,128)S(1)}, pred[6,512]{1,0:T(8,128)(4,1)S(1)...) while((s32[]{:T(128)}, f32[64,256,16]{1,2,0:T(8,128)}, f32[64,256]{1,0:T(8,128)S(1)}, ...), condition=%wide.region_6.7_spmd.clone, body=%wide.region_4.6_spmd.clone.sunk | while | flops 327696384 | bytes 6031468 | solution.py:42
  432.8 1.4 constant_dynamic-slice_fusion.6
  434.1 7.8 fusion.43
  441.9 10.1 %convert_reduce_fusion.2 = f32[64,256]{1,0:T(8,128)S(1)} fusion(s32[512,64]{0,1:T(8,128)S(1)} %dynamic-slice_bitcast_fusion.5, pred[512]{0:T(512)(128)(4,1)S(1)} %dynamic-slice_reduce_fusion.5), kind=kLoop, calls=%fused_computation.17.clone.1 | loop fusion | flops 41926656 | bytes 197120 | tf_op jit(solution)/shard_map/while/body/eval_jaxpr/reduce_sum | solution.py:30
  452.2 1.3 constant_dynamic-slice_fusion.6
  453.5 9.0 %fusion.43 = f32[64,256,16]{1,2,0:T(8,128)} fusion(bf16[512,64,16]{0,2,1:T(8,128)(2,1)S(1)} %bitcast.73, s32[512,64]{0,1:T(8,128)S(1)} %dynamic-slice_bitcast_fusion.5, pred[512]{0:T(512)(128)(4,1)S(1)} %dynamic-slice_reduce_fusion.5, f32[64,256,16]{1,2,0:T(8,128)} %get-tuple-element.262, pred[]{:T(512)S(6)} %compare.6), kind=kOutput, calls=%fused_computation.24.clone.1 | convolution fusion | flops 285736960 | bytes 3277313 | tf_op jit(solution)/shard_map/while/body/eval_jaxpr/bmk,bms->mks/dot_general | solution.py:27
  462.5 10.1 %convert_reduce_fusion.2 = f32[64,256]{1,0:T(8,128)S(1)} fusion(s32[512,64]{0,1:T(8,128)S(1)} %dynamic-slice_bitcast_fusion.5, pred[512]{0:T(512)(128)(4,1)S(1)} %dynamic-slice_reduce_fusion.5), kind=kLoop, calls=%fused_computation.17.clone.1 | loop fusion | flops 41926656 | bytes 197120 | tf_op jit(solution)/shard_map/while/body/eval_jaxpr/reduce_sum | solution.py:30
  472.7 1.3 constant_dynamic-slice_fusion.6
  474.0 9.0 %fusion.43 = f32[64,256,16]{1,2,0:T(8,128)} fusion(bf16[512,64,16]{0,2,1:T(8,128)(2,1)S(1)} %bitcast.73, s32[512,64]{0,1:T(8,128)S(1)} %dynamic-slice_bitcast_fusion.5, pred[512]{0:T(512)(128)(4,1)S(1)} %dynamic-slice_reduce_fusion.5, f32[64,256,16]{1,2,0:T(8,128)} %get-tuple-element.262, pred[]{:T(512)S(6)} %compare.6), kind=kOutput, calls=%fused_computation.24.clone.1 | convolution fusion | flops 285736960 | bytes 3277313 | tf_op jit(solution)/shard_map/while/body/eval_jaxpr/bmk,bms->mks/dot_general | solution.py:27
  483.0 10.1 %convert_reduce_fusion.2 = f32[64,256]{1,0:T(8,128)S(1)} fusion(s32[512,64]{0,1:T(8,128)S(1)} %dynamic-slice_bitcast_fusion.5, pred[512]{0:T(512)(128)(4,1)S(1)} %dynamic-slice_reduce_fusion.5), kind=kLoop, calls=%fused_computation.17.clone.1 | loop fusion | flops 41926656 | bytes 197120 | tf_op jit(solution)/shard_map/while/body/eval_jaxpr/reduce_sum | solution.py:30
  493.3 1.3 constant_dynamic-slice_fusion.6
  494.6 9.0 %fusion.43 = f32[64,256,16]{1,2,0:T(8,128)} fusion(bf16[512,64,16]{0,2,1:T(8,128)(2,1)S(1)} %bitcast.73, s32[512,64]{0,1:T(8,128)S(1)} %dynamic-slice_bitcast_fusion.5, pred[512]{0:T(512)(128)(4,1)S(1)} %dynamic-slice_reduce_fusion.5, f32[64,256,16]{1,2,0:T(8,128)} %get-tuple-element.262, pred[]{:T(512)S(6)} %compare.6), kind=kOutput, calls=%fused_computation.24.clone.1 | convolution fusion | flops 285736960 | bytes 3277313 | tf_op jit(solution)/shard_map/while/body/eval_jaxpr/bmk,bms->mks/dot_general | solution.py:27
  503.6 10.1 %convert_reduce_fusion.2 = f32[64,256]{1,0:T(8,128)S(1)} fusion(s32[512,64]{0,1:T(8,128)S(1)} %dynamic-slice_bitcast_fusion.5, pred[512]{0:T(512)(128)(4,1)S(1)} %dynamic-slice_reduce_fusion.5), kind=kLoop, calls=%fused_computation.17.clone.1 | loop fusion | flops 41926656 | bytes 197120 | tf_op jit(solution)/shard_map/while/body/eval_jaxpr/reduce_sum | solution.py:30
  513.8 1.3 constant_dynamic-slice_fusion.6
  515.1 9.0 %fusion.43 = f32[64,256,16]{1,2,0:T(8,128)} fusion(bf16[512,64,16]{0,2,1:T(8,128)(2,1)S(1)} %bitcast.73, s32[512,64]{0,1:T(8,128)S(1)} %dynamic-slice_bitcast_fusion.5, pred[512]{0:T(512)(128)(4,1)S(1)} %dynamic-slice_reduce_fusion.5, f32[64,256,16]{1,2,0:T(8,128)} %get-tuple-element.262, pred[]{:T(512)S(6)} %compare.6), kind=kOutput, calls=%fused_computation.24.clone.1 | convolution fusion | flops 285736960 | bytes 3277313 | tf_op jit(solution)/shard_map/while/body/eval_jaxpr/bmk,bms->mks/dot_general | solution.py:27
  524.1 10.1 %convert_reduce_fusion.2 = f32[64,256]{1,0:T(8,128)S(1)} fusion(s32[512,64]{0,1:T(8,128)S(1)} %dynamic-slice_bitcast_fusion.5, pred[512]{0:T(512)(128)(4,1)S(1)} %dynamic-slice_reduce_fusion.5), kind=kLoop, calls=%fused_computation.17.clone.1 | loop fusion | flops 41926656 | bytes 197120 | tf_op jit(solution)/shard_map/while/body/eval_jaxpr/reduce_sum | solution.py:30
  534.4 1.3 constant_dynamic-slice_fusion.6
  535.7 9.0 %fusion.43 = f32[64,256,16]{1,2,0:T(8,128)} fusion(bf16[512,64,16]{0,2,1:T(8,128)(2,1)S(1)} %bitcast.73, s32[512,64]{0,1:T(8,128)S(1)} %dynamic-slice_bitcast_fusion.5, pred[512]{0:T(512)(128)(4,1)S(1)} %dynamic-slice_reduce_fusion.5, f32[64,256,16]{1,2,0:T(8,128)} %get-tuple-element.262, pred[]{:T(512)S(6)} %compare.6), kind=kOutput, calls=%fused_computation.24.clone.1 | convolution fusion | flops 285736960 | bytes 3277313 | tf_op jit(solution)/shard_map/while/body/eval_jaxpr/bmk,bms->mks/dot_general | solution.py:27
  544.7 10.1 %convert_reduce_fusion.2 = f32[64,256]{1,0:T(8,128)S(1)} fusion(s32[512,64]{0,1:T(8,128)S(1)} %dynamic-slice_bitcast_fusion.5, pred[512]{0:T(512)(128)(4,1)S(1)} %dynamic-slice_reduce_fusion.5), kind=kLoop, calls=%fused_computation.17.clone.1 | loop fusion | flops 41926656 | bytes 197120 | tf_op jit(solution)/shard_map/while/body/eval_jaxpr/reduce_sum | solution.py:30
  554.9 4.3 copy.37
  559.8 184.6 %all-reduce.4.cloned.1.call-done = (f32[64,4096]{0,1:T(8,128)}, f32[64,256]{1,0:T(8,128)}) async-done(((f32[64,4096]{0,1:T(8,128)}, f32[64,256]{1,0:T(8,128)}), (f32[64,4096]{0,1:T(8,128)}, f32[64,256]{1,0:T(8,128)})) %all-reduce.4.cloned.1.call-update) | async-done | bytes 1114128 | tf_op jit(solution)/shard_map/psum | solution.py:113
  745.3 3.3 fusion.28
  748.6 1.3 copy.42
  750.0 59.4 %while.23 = (s32[]{:T(128)}, f32[6,512]{1,0:T(8,128)S(1)}, pred[6,512]{1,0:T(8,128)(4,1)S(1)}, bf16[6,512,1024]{1,2,0:T(8,128)(2,1)}, s32[6,512,64]{1,2,0:T(8,12...) while((s32[]{:T(128)}, f32[6,512]{1,0:T(8,128)S(1)}, pred[6,512]{1,0:T(8,128)(4,1)S(1)}, ...), condition=%wide.region_11.12_spmd, body=%wide.region_9.11_spmd.sunk | while | flops 287310336 | bytes 4079721 | solution.py:65
  752.5 7.5 fusion.40
  760.1 1.3 constant_dynamic-slice_fusion.5
  762.3 7.5 fusion.40
  772.2 7.5 fusion.40
  782.0 7.5 fusion.40
  791.9 7.5 fusion.40
  799.5 1.3 constant_dynamic-slice_fusion.5
  801.8 7.5 fusion.40
  810.0 1.3 constant_dynamic-slice_fusion.2
  811.3 2.2 copy.44
  813.5 3.1 copy.43
  (90 shorter events, 17.7 us)
Async XLA Ops:
  7.2 97.3 %copy-start = (bf16[1024,1024]{1,0:T(8,128)(2,1)S(1)}, bf16[1024,1024]{1,0:T(8,128)(2,1)}, u32[]{:S(2)}) copy-start(bf16[1024,1024]{1,0:T(8,128)(2,1)} %param.14) | copy-start | bytes 6291460
  88.7 15.7 %all-to-all-start = ((s32[16,1,384]{2,1,0:T(1,128)}), s32[16,1,384]{2,1,0:T(1,128)S(1)}, u32[]{:S(2)}, u32[]{:S(2)}) async-start(s32[16,1,384]{2,1,0:T(1,128)} %bitcast.7), calls=%async_computation | async-start | bytes 49152 | tf_op jit(solution)/shard_map/all_to_all | solution.py:101
  142.1 5.2 copy-start.5
  142.1 238.9 %all-to-all-start.1 = ((bf16[16,384,1024]{2,1,0:T(8,128)(2,1)}), bf16[16,384,1024]{2,1,0:T(8,128)(2,1)}, u32[]{:S(2)}, u32[]{:S(2)}) async-start(bf16[16,384,1024]{2,1,0:T(8,128)(2,1)} %broadcast_select_fusion), calls=%async_computation.1 | async-start | bytes 25165824 | tf_op jit(solution)/shard_map/all_to_all | solution.py:104
  147.2 597.2 %all-reduce.4.cloned.1.call-start = ((), (), s32[]{:S(2)}) async-start(), calls=%async_computation.2 | async-start | bytes 4325376 | tf_op jit(solution)/shard_map/psum | solution.py:113
  432.7 126.5 %copy-start.4 = (f32[64,4096]{1,0:T(8,128)S(1)}, f32[64,4096]{1,0:T(8,128)}, u32[]{:S(2)}) copy-start(f32[64,4096]{1,0:T(8,128)} %param.15) | copy-start | bytes 3145732
  554.9 4.3 copy-start.3
  554.9 4.3 copy-start.2
  809.4 7.3 copy-start.1
Sparse Core Ops, SparseCore 0:
  559.3 185.0 all-reduce.3
where the time goes:
time: 825 us; the launch traced here: 824 us
  waiting for transfers between devices  426 us (52%)
  local copies, waits for them, and re-layouts  177 us (21%)
  matrix products  97.9 us (12%)
  other arithmetic  94.3 us (11%)
  between operations  15.1 us (2%)
  starting transfers between devices  13.5 us (2%)
    all_to_all x1, waiting for transfers between devices, body(): lax.all_to_all(found, 'wide', split_axis=0, concat_axis=0, tiled=True)  234 us
    psum x1, waiting for transfers between devices, body(): sums, counts = lax.psum((sums, counts), ('narrow', 'wide'))  185 us
    reduce_sum x6, other arithmetic, absorb(): counts = carry[1] + jnp.sum(onehot, axis=0, dtype=jnp.float32)  60.8 us
    gather x1, local copies, waits for them, and re-layouts, body(): send_lists = padded_lists[source_row].reshape(wide_count, capacity)  60.6 us
    dot_general x6, matrix products, absorb(): jnp.einsum('bmk,bms->mks', onehot, shaped, preferred_element_type=jnp.flo...  52.9 us
    dot_general x6, matrix products, measure(): jnp.einsum('bmk,mks->bms', onehot, table, preferred_element_type=jnp.floa...  45 us
    gather x1, local copies, waits for them, and re-layouts, body(): centroids[wanted]  26.8 us
    gather x1, local copies, waits for them, and re-layouts, body(): padded_fetch[slot_of_row].astype(jnp.float32)  22.2 us
  transfers between devices with their start and end apart: 3, of which 3 were waited for; matrix products, arithmetic and copies ran while one was open for 0% of the time, Pallas kernels for 0%

commit v1 on v0

v1 whole, which is shorter than its diff:
```python
import functools

import jax
import jax.numpy as jnp
from jax import lax
from jax.experimental import pallas as pl
from jax.experimental.pallas import tpu as pltpu
from jax.sharding import PartitionSpec as P

K = 256
LO = 4
HI = K // LO
CHUNKS = 1
BLOCK = 512
VMEM = 56 * 1024 * 1024


def sums_kernel(lanes, rows_ref, cent_ref, hi_ref, low_ref, spread_ref, resid_ref, sums_ref, counts_ref, acc_ref, cacc_ref):
    step = pl.program_id(0)
    width = rows_ref.shape[1]
    spaces = hi_ref.shape[0]
    per = lanes // (width // spaces)
    block = rows_ref.shape[0]

    @pl.when(step == 0)
    def _():
        acc_ref[...] = jnp.zeros_like(acc_ref)
        cacc_ref[...] = jnp.zeros_like(cacc_ref)

    resid = (rows_ref[...].astype(jnp.float32) - cent_ref[...].astype(jnp.float32)).astype(jnp.bfloat16)
    resid_ref[...] = resid
    low = jnp.dot(low_ref[...], spread_ref[...], preferred_element_type=jnp.float32)
    level = lax.broadcasted_iota(jnp.int32, (HI, block), 0)
    zero = jnp.zeros((), jnp.bfloat16)
    for g in range(width // lanes):
        part = resid[:, g * lanes : (g + 1) * lanes]
        part_low = low[:, g * lanes : (g + 1) * lanes].astype(jnp.bfloat16)
        right = jnp.concatenate(
            [jnp.where(part_low == jnp.bfloat16(j), part, zero) for j in range(LO)], axis=1
        )
        left = jnp.concatenate(
            [
                (hi_ref[m : m + 1, :] == level).astype(jnp.float32).astype(jnp.bfloat16)
                for m in range(g * per, (g + 1) * per)
            ],
            axis=0,
        )
        acc_ref[g] += jnp.dot(left, right, preferred_element_type=jnp.float32)
        cacc_ref[g] += jnp.dot(left, low_ref[...], preferred_element_type=jnp.float32)

    @pl.when(step == pl.num_programs(0) - 1)
    def _():
        sub = lanes // per
        own = lax.broadcasted_iota(jnp.int32, (HI, lanes), 1) // sub
        for g in range(width // lanes):
            for j in range(LO):
                total = jnp.zeros((HI, lanes), jnp.float32)
                for m in range(per):
                    piece = acc_ref[g, m * HI : (m + 1) * HI, j * lanes : (j + 1) * lanes]
                    total = total + jnp.where(own == m, piece, 0.0)
                sums_ref[j * HI : (j + 1) * HI, g * lanes : (g + 1) * lanes] = total
        space = lax.broadcasted_iota(jnp.int32, (HI, LO * spaces), 1) % spaces
        total = jnp.zeros((HI, LO * spaces), jnp.float32)
        for g in range(width // lanes):
            for m in range(per):
                piece = cacc_ref[g, m * HI : (m + 1) * HI, :]
                total = total + jnp.where(space == g * per + m, piece, 0.0)
        counts_ref[...] = total


def error_kernel(lanes, resid_ref, hi_ref, low_ref, spread_ref, widen_ref, table_ref, err_ref, diag_ref):
    step = pl.program_id(0)
    width = resid_ref.shape[1]
    spaces = hi_ref.shape[1]
    sub = width // spaces
    per = lanes // sub
    block = resid_ref.shape[0]

    @pl.when(step == 0)
    def _():
        own = lax.broadcasted_iota(jnp.int32, (HI, lanes), 1) // sub
        for g in range(width // lanes):
            for j in range(LO):
                piece = table_ref[j * HI : (j + 1) * HI, g * lanes : (g + 1) * lanes].astype(jnp.float32)
                for m in range(per):
                    diag_ref[g, m * HI : (m + 1) * HI, j * lanes : (j + 1) * lanes] = jnp.where(
                        own == m, piece, 0.0
                    ).astype(jnp.bfloat16)

    low = jnp.dot(low_ref[...], spread_ref[...], preferred_element_type=jnp.float32)
    level = (lax.broadcasted_iota(jnp.int32, (block, per * HI), 1) % HI).astype(jnp.float32)
    total = jnp.zeros((block, lanes), jnp.float32)
    for g in range(width // lanes):
        high = jnp.dot(
            hi_ref[...], widen_ref[:, g * per * HI : (g + 1) * per * HI], preferred_element_type=jnp.float32
        )
        pick = (high == level).astype(jnp.float32).astype(jnp.bfloat16)
        words = jnp.dot(pick, diag_ref[g], preferred_element_type=jnp.float32)
        part_low = low[:, g * lanes : (g + 1) * lanes]
        decoded = words[:, :lanes]
        for j in range(1, LO):
            decoded = jnp.where(part_low == float(j), words[:, j * lanes : (j + 1) * lanes], decoded)
        diff = resid_ref[:, g * lanes : (g + 1) * lanes].astype(jnp.float32) - decoded
        total = total + diff * diff
    err_ref[0] = jnp.sum(total.T, axis=0, keepdims=True)


def codeword_sums(rows, cent, hi_cols, low_hot, spread):
    total, width = rows.shape
    spaces = hi_cols.shape[0]
    lanes = min(128, width)
    per = lanes // (width // spaces)
    groups = width // lanes
    row_block = pl.BlockSpec((BLOCK, width), lambda i: (i, 0))
    return pl.pallas_call(
        functools.partial(sums_kernel, lanes),
        grid=(total // BLOCK,),
        in_specs=[
            row_block,
            row_block,
            pl.BlockSpec((spaces, BLOCK), lambda i: (0, i)),
            pl.BlockSpec((BLOCK, LO * spaces), lambda i: (i, 0)),
            pl.BlockSpec((LO * spaces, width), lambda i: (0, 0)),
        ],
        out_specs=[
            row_block,
            pl.BlockSpec((K, width), lambda i: (0, 0)),
            pl.BlockSpec((HI, LO * spaces), lambda i: (0, 0)),
        ],
        out_shape=[
            jax.ShapeDtypeStruct((total, width), jnp.bfloat16),
            jax.ShapeDtypeStruct((K, width), jnp.float32),
            jax.ShapeDtypeStruct((HI, LO * spaces), jnp.float32),
        ],
        scratch_shapes=[
            pltpu.VMEM((groups, per * HI, LO * lanes), jnp.float32),
            pltpu.VMEM((groups, per * HI, LO * spaces), jnp.float32),
        ],
        compiler_params=pltpu.CompilerParams(vmem_limit_bytes=VMEM),
        cost_estimate=pl.CostEstimate(
            flops=2 * total * per * HI * LO * width, bytes_accessed=6 * total * width, transcendentals=0
        ),
        name="codeword_sums",
    )(rows, cent, hi_cols, low_hot, spread)


def squared_errors(resid, hi_rows, low_hot, spread, widen, table):
    total, width = resid.shape
    spaces = hi_rows.shape[1]
    lanes = min(128, width)
    per = lanes // (width // spaces)
    groups = width // lanes
    whole = lambda a: pl.BlockSpec(a.shape, lambda i: (0, 0))
    return pl.pallas_call(
        functools.partial(error_kernel, lanes),
        grid=(total // BLOCK,),
        in_specs=[
            pl.BlockSpec((BLOCK, width), lambda i: (i, 0)),
            pl.BlockSpec((BLOCK, spaces), lambda i: (i, 0)),
            pl.BlockSpec((BLOCK, LO * spaces), lambda i: (i, 0)),
            whole(spread),
            whole(widen),
            whole(table),
        ],
        out_specs=pl.BlockSpec((1, 1, BLOCK), lambda i: (i, 0, 0)),
        out_shape=jax.ShapeDtypeStruct((total // BLOCK, 1, BLOCK), jnp.float32),
        scratch_shapes=[pltpu.VMEM((groups, per * HI, LO * lanes), jnp.bfloat16)],
        compiler_params=pltpu.CompilerParams(vmem_limit_bytes=VMEM),
        cost_estimate=pl.CostEstimate(
            flops=2 * total * per * HI * LO * width, bytes_accessed=2 * total * width, transcendentals=0
        ),
        name="squared_errors",
    )(resid, hi_rows, low_hot, spread, widen, table).reshape(total)


def body(rows, list_ids, codes, row_counts, centroids, old_codebook):
    local_rows, width_d = rows.shape
    spaces = codes.shape[1]
    sub = width_d // spaces
    wide_count = lax.axis_size("wide")
    narrow_count = lax.axis_size("narrow")
    core = lax.axis_index("narrow")
    own_wide = lax.axis_index("wide")
    anchor = float(local_rows * narrow_count * wide_count // (4 * K))
    half = width_d // narrow_count
    half_spaces = spaces // narrow_count
    swap = [(0, 1), (1, 0)]

    mine = lambda a, n: lax.dynamic_slice_in_dim(a, core * n, n, 1)
    others = lambda a, n: lax.dynamic_slice_in_dim(a, (1 - core) * n, n, 1)
    width = half // CHUNKS
    chunk_spaces = half_spaces // CHUNKS
    own_cent = mine(centroids, half)
    gathered = [
        lax.all_gather(own_cent[:, c * width : (c + 1) * width], "wide", axis=0, tiled=True) for c in range(CHUNKS)
    ]

    is_live = jnp.arange(local_rows, dtype=jnp.int32) < row_counts[0]
    keyed = jnp.where(is_live[:, None], codes, 4 * K)
    both_rows = jnp.concatenate([mine(rows, half), lax.ppermute(others(rows, half), "narrow", swap)])
    both_codes = jnp.concatenate(
        [mine(keyed, half_spaces), lax.ppermute(others(keyed, half_spaces), "narrow", swap)]
    )
    both_lists = jnp.concatenate([list_ids, lax.ppermute(list_ids, "narrow", swap)])
    total = both_rows.shape[0]
    hi = both_codes // LO
    low = both_codes % LO
    old = mine(old_codebook.reshape(1, spaces, HI, LO, sub), half_spaces)
    old = old.reshape(half_spaces, HI, LO, sub).transpose(2, 1, 0, 3).reshape(K, half)

    feature = jnp.arange(width, dtype=jnp.int32) // sub
    space = jnp.arange(chunk_spaces, dtype=jnp.int32)
    expand = (feature[None, :] == space[:, None]).astype(jnp.float32)
    level = jnp.arange(LO, dtype=jnp.float32)
    spread = (level[:, None, None] * expand[None]).reshape(LO * chunk_spaces, width).astype(jnp.bfloat16)
    widen = jnp.repeat(jnp.eye(chunk_spaces, dtype=jnp.bfloat16), HI, axis=1)

    errs = jnp.zeros((total,), jnp.float32)
    books = []
    for c in range(CHUNKS):
        cols = slice(c * width, (c + 1) * width)
        spc = slice(c * chunk_spaces, (c + 1) * chunk_spaces)
        low_hot = (low[:, None, spc] == jnp.arange(LO, dtype=jnp.int32)[None, :, None]).astype(jnp.bfloat16)
        low_hot = low_hot.reshape(total, LO * chunk_spaces)
        cent = gathered[c].at[both_lists].get(mode="clip")
        resid, sums, counts = codeword_sums(both_rows[:, cols], cent, hi[:, spc].T, low_hot, spread)
        sums, counts = lax.psum((sums, counts), "wide")
        counts = counts.reshape(HI, LO, chunk_spaces).transpose(1, 0, 2).reshape(K, chunk_spaces)
        weight = jnp.dot(counts + anchor, expand, precision=lax.Precision.HIGHEST)
        book = (sums + anchor * old[:, cols]) / weight
        errs = errs + squared_errors(
            resid, hi[:, spc].astype(jnp.bfloat16), low_hot, spread, widen, book.astype(jnp.bfloat16)
        )
        books.append(book)
    book = jnp.concatenate(books, axis=1) if CHUNKS > 1 else books[0]
    book = book.reshape(LO, HI, half_spaces, sub).transpose(2, 1, 0, 3).reshape(half_spaces, K * sub)
    codebook = lax.all_gather(book, "narrow", axis=0, tiled=True)
    share = spaces // wide_count
    search_table = lax.dynamic_slice_in_dim(codebook, own_wide * share, share, 0).astype(jnp.bfloat16)
    err = errs[:local_rows] + lax.ppermute(errs[local_rows:], "narrow", swap)
    err = jnp.where(is_live, err / width_d, 0.0)
    return (codebook, search_table, err)


def solution(mesh):
    in_specs = (
        P(("narrow", "wide"), None),
        P(("narrow", "wide")),
        P(("narrow", "wide"), None),
        P(("narrow", "wide")),
        P("wide", None),
        P(),
    )
    out_specs = (P(), P("wide", None), P(("narrow", "wide")))
    return jax.shard_map(body, mesh=mesh, in_specs=in_specs, out_specs=out_specs, check_vma=False)
```

time: 825 us -> 420 us (0.51)
  waiting for transfers between devices: 426 us -> 182 us
  local copies, waits for them, and re-layouts: 177 us -> 70.7 us
  matrix products: 97.9 us -> 0.42 us
  blocking collectives: 0 us -> 74.1 us
  other arithmetic: 94.3 us -> 22.2 us
  Pallas kernels: 0 us -> 54.7 us
  starting transfers between devices: 13.5 us -> 1.22 us
    all_to_all x2 -> x0, waiting for transfers between devices: 241 us -> none  [the longest x1 234 us: body(): lax.all_to_all(found, 'wide', split_axis=0, concat_axis=0, tiled=True)]
    psum x1, waiting for transfers between devices: 185 us -> 28.1 us  [body(): sums, counts = lax.psum((sums, counts), 'wide')]
    all_gather x0 -> x2, waiting for transfers between devices: none -> 152 us  [the longest x1 152 us: body(): lax.all_gather(own_cent[:, c * width:(c + 1) * width], 'wide', axis=0, ti...]
    dot_general x12 -> x1, matrix products: 97.9 us -> 0.42 us  [body(): weight = jnp.dot(counts + anchor, expand, precision=lax.Precision.HIGHEST)]
    gather x3 -> x1, local copies, waits for them, and re-layouts: 110 us -> 33.5 us  [body(): cent = gathered[c].at[both_lists].get(mode='clip')]
    psum x0 -> x1, blocking collectives: none -> 74.1 us  [body(): sums, counts = lax.psum((sums, counts), 'wide')]
    reduce_sum x7 -> x0, other arithmetic: 60.9 us -> none  [the longest x6 60.8 us: absorb(): counts = carry[1] + jnp.sum(onehot, axis=0, dtype=jnp.float32)]
    pallas_call x0 -> x2, Pallas kernels: none -> 54.7 us  [the longest x1 27.9 us: codeword_sums(): pl.pallas_call(functools.partial(sums_kernel, lanes), grid=(total // BLOC...]
  transfers between devices with their start and end apart: 3 -> 7, of which waited for: 3 -> 3; matrix products, arithmetic and copies ran while one was open for 0% -> 11% of each run, Pallas kernels for 0% -> 6%
where the time goes in v1:
time: 420 us; the launch traced here: 419 us
  waiting for transfers between devices  182 us (43%)
  blocking collectives  74.1 us (18%)
  local copies, waits for them, and re-layouts  70.7 us (17%)
  Pallas kernels  54.7 us (13%)
  other arithmetic  22.2 us (5%)
  between operations  14.6 us (3%)
    all_gather x1, waiting for transfers between devices, body(): lax.all_gather(own_cent[:, c * width:(c + 1) * width], 'wide', axis=0, ti...  152 us
    psum x1, blocking collectives, body(): sums, counts = lax.psum((sums, counts), 'wide')  74.1 us
    gather x1, local copies, waits for them, and re-layouts, body(): cent = gathered[c].at[both_lists].get(mode='clip')  33.5 us
    psum x1, waiting for transfers between devices, body(): sums, counts = lax.psum((sums, counts), 'wide')  28.1 us
    pallas_call x1, Pallas kernels, codeword_sums(): pl.pallas_call(functools.partial(sums_kernel, lanes), grid=(total // BLOC...  27.9 us
    pallas_call x1, Pallas kernels, squared_errors(): pl.pallas_call(functools.partial(error_kernel, lanes), grid=(total // BLO...  26.8 us
  transfers between devices with their start and end apart: 7, of which 3 were waited for; matrix products, arithmetic and copies ran while one was open for 11% of the time, Pallas kernels for 6%

profile of v1, /device:TPU:0, one launch (start us, length us, event | category | flops | bytes accessed | tf_op | source)
XLA Modules:
  0.0 419.4 jit_solution(14229424345092620441)
XLA Ops:
  7.3 1.5 copy-done
  8.8 1.1 constant_dynamic-slice_fusion.2
  9.9 0.0 all-reduce.2.cloned.1.call-start
  9.9 0.5 collective-permute-start.1
  11.1 0.1 broadcast_select_fusion
  11.2 0.1 constant_dynamic-slice_fusion.1
  11.3 0.1 collective-permute-start.2
  11.4 6.0 %constant_dynamic-slice_fusion.4 = (bf16[3072,512]{1,0:T(8,128)(2,1)}, bf16[3072,512]{1,0:T(8,128)(2,1)}) fusion(bf16[3072,1024]{1,0:T(8,128)(2,1)} %param.6, s32[]{:T(128)S(6)} %select_n.64, s32[]{:T(128)S(6)} %select_n.65), kind=kLoop, calls=%fused_computation.40 | loop fusion | bytes 12582920 | tf_op jit(solution)/shard_map/dynamic_slice | solution.py:189
  17.4 0.5 collective-permute-start
  17.8 1.9 copy.33
  19.7 2.2 multiply_bitcast_fusion
  22.0 0.1 mul.69
  22.1 0.1 eq.57
  22.1 0.7 fusion.2.spread_ref
  22.9 0.8 copy-done.5
  23.7 1.1 pad_add_fusion
  24.8 2.4 copy.26
  27.1 7.1 %fusion.10 = (bf16[6144,32]{1,0:T(8,128)(2,1)}, s32[6144,32]{1,0:T(8,128)}, s32[32,6144]{0,1:T(8,128)}) fusion(s32[6144,32]{1,0:T(8,128)} %copy.26), kind=kLoop, calls=%fused_computation.41 | loop fusion | flops 3932160 | bytes 2752512 | tf_op jit(solution)/shard_map/convert_element_type | solution.py:232
  34.2 2.3 copy.30
  36.5 3.1 copy.32.hi_ref
  39.6 1.9 eq.54
  41.6 3.6 copy.31
  45.1 3.5 compare_convert_fusion.low_ref
  48.6 5.0 %pad_maximum_fusion.rows_ref = bf16[6144,512]{1,0:T(8,128)(2,1)} fusion(bf16[3072,512]{1,0:T(8,128)(2,1)} %collective-permute-done, bf16[3072,512]{1,0:T(8,128)(2,1)S(1)} %copy-done.2), kind=kLoop, calls=%fused_computation.1 | loop fusion | flops 12582912 | bytes 12582912 | tf_op jit(solution)/shard_map/concatenate | solution.py:200
  53.6 152.2 %all-gather.3.cloned.1.call-done = bf16[16384,512]{1,0:T(8,128)(2,1)} async-done(((bf16[1024,512]{1,0:T(8,128)(2,1)}), bf16[16384,512]{1,0:T(8,128)(2,1)}) %all-gather.3.cloned.1.call-update) | async-done | bytes 16777232 | tf_op jit(solution)/shard_map/all_gather | solution.py:195
  205.7 33.5 %gather_fusion = bf16[6144,512]{1,0:T(8,128)(2,1)} fusion(bf16[16384,512]{1,0:T(8,128)(2,1)} %all-gather.3.cloned.1.call-done, s32[6144]{0:T(1024)S(1)} %broadcast_clamp_fusion), kind=kCustom, calls=%fused_computation | custom fusion | bytes 12607488 | tf_op jit(solution)/shard_map/gather | solution.py:225
  239.3 27.9 %codeword_sums.1 = (bf16[6144,512]{1,0:T(8,128)(2,1)}, f32[256,512]{1,0:T(8,128)}, f32[64,128]{1,0:T(8,128)}) custom-call(bf16[6144,512]{1,0:T(8,128)(2,1)} %pad_maximum_fusion.rows_ref, bf16[6144,512]{1,0:T(8,128)(2,1)} %gather_fusion, s32[32,6144]{1,0:T(8,128)} %copy.32.hi_ref, bf16[6144,128]{1,0:T(8,128)(2,1)} %compare_convert_fusion.low_ref, ...), custom_call_target="tpu_custom_call" | custom-call | flops 12884901888 | bytes 18874368 | tf_op jit(solution)/shard_map/codeword_sums/pallas_call | solution.py:115
  267.2 0.2 broadcast_in_dim.29
  267.5 0.9 reshape.212.widen_ref
  268.4 1.7 copy.34
  270.1 0.6 mul.78
  270.7 0.2 copy.35
  271.0 74.1 %psum.15 = f32[64,128]{1,0:T(8,128)S(1)} all-reduce(f32[64,128]{1,0:T(8,128)S(1)} %copy-done.6), channel_id=1, replica_groups=mesh['narrow'=2,'wide'=16] {'wide'}, use_global_device_ids=true, to_apply=%region_1.2 | all-reduce | flops 8192 | bytes 65536 | tf_op jit(solution)/shard_map/psum | solution.py:227
  345.0 0.1 copy.36
  345.2 0.1 add.83
  345.3 0.4 fusion.3
  345.7 28.1 %all-reduce.2.cloned.1.call-done = f32[256,512]{1,0:T(8,128)} async-done(((f32[256,512]{1,0:T(8,128)}), f32[256,512]{1,0:T(8,128)}) %all-reduce.2.cloned.1.call-update) | async-done | bytes 524304 | tf_op jit(solution)/shard_map/psum | solution.py:227
  373.8 1.9 fusion.12
  375.8 0.2 copy.38
  376.0 0.5 reshape.210
  376.4 1.9 copy.39
  378.3 1.4 copy.40
  379.7 26.8 %squared_errors.1 = f32[12,1,512]{2,1,0:T(1,128)} custom-call(bf16[6144,512]{1,0:T(8,128)(2,1)} %get-tuple-element.8.resid_ref, bf16[6144,32]{1,0:T(8,128)(2,1)} %get-tuple-element.16.hi_ref, bf16[6144,128]{1,0:T(8,128)(2,1)} %compare_convert_fusion.low_ref, bf16[128,512]{1,0:T(8,128)(2,1)} %fusion.2.spread_ref, bf16[32,2048]{1,0:T(8,128)(2,1)} %reshape.212.widen_ref, ...), custom_call_target="tpu_custom_call" | custom-call | flops 12884901888 | bytes 6291456 | tf_op jit(solution)/shard_map/squared_errors/pallas_call | solution.py:154
  406.5 0.7 fusion.13
  407.3 1.2 collective-permute-done.3
  408.4 0.6 multiply_select_fusion
  409.0 1.5 dynamic-slice_convert_fusion
  410.6 2.3 copy.44
  (34 shorter events, 0.3 us)
Async XLA Ops:
  7.2 1.6 copy-start
  7.2 2.7 copy-start.7
  7.2 3.9 copy-start.4
  7.2 198.5 %all-gather.3.cloned.1.call-start = ((), (), s32[]{:S(2)}) async-start(), calls=%async_computation | async-start | bytes 17825792 | tf_op jit(solution)/shard_map/all_gather | solution.py:195
  9.9 364.0 %all-reduce.2.cloned.1.call-start = ((), (), s32[]{:S(2)}) async-start(), calls=%async_computation.1 | async-start | bytes 1048576 | tf_op jit(solution)/shard_map/psum | solution.py:227
  9.9 13.0 %collective-permute-start.1 = (s32[3072]{0:T(1024)S(1)}, s32[3072]{0:T(1024)S(1)}, u32[]{:S(2)}, u32[]{:S(2)}) collective-permute-start(s32[3072]{0:T(1024)S(1)} %copy-done.7), channel_id=1, source_target_pairs={{0,16},{16,0},{1,17},{17,1},{2,18},{18,2},{3,19},{19,3},{4,20},{20... | collective-permute-start | bytes 36872 | tf_op jit(solution)/shard_map/ppermute | solution.py:204
  11.3 11.7 %collective-permute-start.2 = (s32[3072,32]{0,1:T(8,128)S(1)}, s32[3072,32]{0,1:T(8,128)S(1)}, u32[]{:S(2)}, u32[]{:S(2)}) collective-permute-start(s32[3072,32]{0,1:T(8,128)S(1)} %get-tuple-element.20), channel_id=1, source_target_pairs={{0,16},{16,0},{1,17},{17,1},{2,18},{18,2},{3,19},{19,3},{4,20},{20... | collective-permute-start | bytes 1179656 | tf_op jit(solution)/shard_map/ppermute | solution.py:202
  11.4 6.4 %copy-start.3 = (f32[64,4096]{1,0:T(8,128)S(1)}, f32[64,4096]{1,0:T(8,128)}, u32[]{:S(2)}) copy-start(f32[64,4096]{1,0:T(8,128)} %param.11) | copy-start | bytes 3145732
  17.4 31.3 %collective-permute-start = (bf16[3072,512]{1,0:T(8,128)(2,1)}, bf16[3072,512]{1,0:T(8,128)(2,1)}, u32[]{:S(2)}, u32[]{:S(2)}) collective-permute-start(bf16[3072,512]{1,0:T(8,128)(2,1)} %get-tuple-element.15), channel_id=1, source_target_pairs={{0,16},{16,0},{1,17},{17,1},{2,18},{18,2},{3,19},{19,3},{4,20},{20... | collective-permute-start | bytes 9437192 | tf_op jit(solution)/shard_map/ppermute | solution.py:200
  22.9 0.8 copy-start.5
  45.1 3.5 copy-start.2
  267.2 141.9 %all-gather.5.cloned.1.call-start = ((), (), s32[]{:S(2)}) async-start(), calls=%async_computation.2 | async-start | bytes 1572864 | tf_op jit(solution)/shard_map/all_gather | solution.py:237
  267.4 3.5 copy-start.6
  379.7 33.1 %copy-start.1 = (bf16[1024,1024]{1,0:T(8,128)(2,1)S(1)}, bf16[1024,1024]{1,0:T(8,128)(2,1)}, u32[]{:S(2)}) copy-start(bf16[1024,1024]{1,0:T(8,128)(2,1)} %param.10) | copy-start | bytes 6291460
  407.3 1.2 collective-permute-start.3
Sparse Core Ops, SparseCore 0:
  11.4 194.3 all-gather.2
  267.3 106.4 all-reduce.1
  379.8 7.9 all-gather.4

commit v2 on v1

--- a/solution.py
+++ b/solution.py
@@ -105,6 +105,91 @@
     err_ref[0] = jnp.sum(total.T, axis=0, keepdims=True)
 
 
+def reduce_kernel(n, x_ref, out_ref, got, full, send1, recv1, send2, recv2):
+    me = lax.axis_index("wide")
+    core = lax.axis_index("narrow")
+    barrier = pltpu.get_barrier_semaphore()
+
+    def greet(k, _):
+        pl.semaphore_signal(
+            barrier, inc=1, device_id=(core, lax.rem(me + k, n)), device_id_type=pl.DeviceIdType.MESH
+        )
+        return 0
+
+    lax.fori_loop(1, n, greet, 0)
+    pl.semaphore_wait(barrier, n - 1)
+
+    def part(k):
+        peer = lax.rem(me + k, n)
+        return pltpu.make_async_remote_copy(
+            src_ref=x_ref.at[peer],
+            dst_ref=got.at[k],
+            send_sem=send1.at[k],
+            recv_sem=recv1.at[k],
+            device_id=(core, peer),
+            device_id_type=pl.DeviceIdType.MESH,
+        )
+
+    def share(k, slot):
+        return pltpu.make_async_remote_copy(
+            src_ref=full.at[slot],
+            dst_ref=full.at[slot],
+            send_sem=send2.at[k],
+            recv_sem=recv2.at[k],
+            device_id=(core, lax.rem(me + k, n)),
+            device_id_type=pl.DeviceIdType.MESH,
+        )
+
+    def each(act):
+        def step(k, _):
+            act(k)
+            return 0
+
+        lax.fori_loop(1, n, step, 0)
+
+    each(lambda k: part(k).start())
+
+    def add(k, total):
+        part(k).wait_recv()
+        return total + got[k]
+
+    full[me] = lax.fori_loop(1, n, add, x_ref[me])
+    each(lambda k: share(k, me).start())
+    each(lambda k: share(k, lax.rem(me - k + n, n)).wait_recv())
+    each(lambda k: part(k).wait_send())
+    each(lambda k: share(k, me).wait_send())
+    out_ref[...] = full[...]
+
+
+def reduce_wide(sums, counts, n):
+    width = sums.shape[1]
+    rows_s, rows_c = sums.shape[0] // n, counts.shape[0] // n
+    pad = -(rows_s + rows_c) % 8
+    counts_in = jnp.pad(
+        counts.reshape(n, rows_c, counts.shape[1]), ((0, 0), (0, pad), (0, width - counts.shape[1]))
+    )
+    parts = jnp.concatenate([sums.reshape(n, rows_s, width), counts_in], axis=1)
+    full = pl.pallas_call(
+        functools.partial(reduce_kernel, n),
+        out_shape=jax.ShapeDtypeStruct(parts.shape, parts.dtype),
+        in_specs=[pl.BlockSpec(memory_space=pltpu.VMEM)],
+        out_specs=pl.BlockSpec(memory_space=pltpu.VMEM),
+        scratch_shapes=[
+            pltpu.VMEM(parts.shape, parts.dtype),
+            pltpu.VMEM(parts.shape, parts.dtype),
+        ]
+        + [pltpu.SemaphoreType.DMA((n,))] * 4,
+        compiler_params=pltpu.CompilerParams(
+            collective_id=0, has_side_effects=True, vmem_limit_bytes=24 * 1024 * 1024
+        ),
+        name="reduce_wide",
+    )(parts)
+    return (
+        full[:, :rows_s].reshape(sums.shape),
+        full[:, rows_s : rows_s + rows_c, : counts.shape[1]].reshape(counts.shape),
+    )
+
+
 def codeword_sums(rows, cent, hi_cols, low_hot, spread):
     total, width = rows.shape
     spaces = hi_cols.shape[0]
@@ -224,7 +309,7 @@
         low_hot = low_hot.reshape(total, LO * chunk_spaces)
         cent = gathered[c].at[both_lists].get(mode="clip")
         resid, sums, counts = codeword_sums(both_rows[:, cols], cent, hi[:, spc].T, low_hot, spread)
-        sums, counts = lax.psum((sums, counts), "wide")
+        sums, counts = reduce_wide(sums, counts, wide_count)
         counts = counts.reshape(HI, LO, chunk_spaces).transpose(1, 0, 2).reshape(K, chunk_spaces)
         weight = jnp.dot(counts + anchor, expand, precision=lax.Precision.HIGHEST)
         book = (sums + anchor * old[:, cols]) / weight

time: 420 us -> 353 us (0.84)
  blocking collectives: 74.1 us -> 0 us
  Pallas kernels: 54.7 us -> 92.3 us
  waiting for transfers between devices: 182 us -> 146 us
    psum x1 -> x0, blocking collectives: 74.1 us -> none  [body(): sums, counts = lax.psum((sums, counts), 'wide')]
    pallas_call x0 -> x1, Pallas kernels: none -> 37.7 us  [reduce_wide(): pl.pallas_call(functools.partial(reduce_kernel, n), out_shape=jax.ShapeDt...]
    psum x1 -> x0, waiting for transfers between devices: 28.1 us -> none  [body(): sums, counts = lax.psum((sums, counts), 'wide')]
    all_gather x1, waiting for transfers between devices: 152 us -> 145 us  [body(): lax.all_gather(own_cent[:, c * width:(c + 1) * width], 'wide', axis=0, ti...]
  transfers between devices with their start and end apart: 7 -> 6, of which waited for: 3 -> 2; matrix products, arithmetic and copies ran while one was open for 11% -> 14% of each run, Pallas kernels for 6% -> 8%
where the time goes in v2:
time: 353 us; the launch traced here: 352 us
  waiting for transfers between devices  146 us (41%)
  Pallas kernels  92.3 us (26%)
  local copies, waits for them, and re-layouts  71.8 us (20%)
  other arithmetic  23.9 us (7%)
  between operations  14.9 us (4%)
    all_gather x1, waiting for transfers between devices, body(): lax.all_gather(own_cent[:, c * width:(c + 1) * width], 'wide', axis=0, ti...  145 us
    pallas_call x1, Pallas kernels, reduce_wide(): pl.pallas_call(functools.partial(reduce_kernel, n), out_shape=jax.ShapeDt...  37.7 us
    gather x1, local copies, waits for them, and re-layouts, body(): cent = gathered[c].at[both_lists].get(mode='clip')  33.6 us
    pallas_call x1, Pallas kernels, codeword_sums(): pl.pallas_call(functools.partial(sums_kernel, lanes), grid=(total // BLOC...  27.9 us
    pallas_call x1, Pallas kernels, squared_errors(): pl.pallas_call(functools.partial(error_kernel, lanes), grid=(total // BLO...  26.7 us
    dynamic_slice x3, local copies, waits for them, and re-layouts, body(): mine = lambda a, n: lax.dynamic_slice_in_dim(a, core * n, n, 1)  7.87 us
    convert_element_type x1, other arithmetic, body(): hi[:, spc].astype(jnp.bfloat16)  7.08 us
  transfers between devices with their start and end apart: 6, of which 2 were waited for; matrix products, arithmetic and copies ran while one was open for 14% of the time, Pallas kernels for 8%

profile of v2, /device:TPU:0, one launch (start us, length us, event | category | flops | bytes accessed | tf_op | source)
XLA Modules:
  0.0 351.6 jit_solution(2947678073639998221)
XLA Ops:
  7.3 1.5 copy-done
  8.8 1.1 constant_dynamic-slice_fusion.2
  9.9 0.5 collective-permute-start.1
  11.1 0.1 broadcast_select_fusion
  11.2 0.8 constant_dynamic-slice_fusion.1
  12.1 6.0 %constant_dynamic-slice_fusion.4 = (bf16[3072,512]{1,0:T(8,128)(2,1)}, bf16[3072,512]{1,0:T(8,128)(2,1)}) fusion(bf16[3072,1024]{1,0:T(8,128)(2,1)} %param.6, s32[]{:T(128)S(6)} %select_n.64, s32[]{:T(128)S(6)} %select_n.65), kind=kLoop, calls=%fused_computation.42 | loop fusion | bytes 12582920 | tf_op jit(solution)/shard_map/dynamic_slice | solution.py:274
  18.0 0.5 collective-permute-start
  18.5 1.9 copy.32
  20.4 2.3 multiply_bitcast_fusion
  22.7 0.6 fusion.3
  23.4 0.6 mul.69
  24.0 0.6 eq.57
  24.6 0.2 broadcast_in_dim.29
  24.8 0.9 reshape.223.widen_ref
  25.7 1.7 copy.33
  27.5 0.6 mul.78
  28.1 0.2 copy.34
  28.3 1.6 fusion.2.spread_ref
  29.9 0.7 compare_select_fusion
  30.6 1.1 pad_add_fusion
  31.7 2.2 copy.25
  33.9 7.1 %fusion.9 = (bf16[6144,32]{1,0:T(8,128)(2,1)}, s32[6144,32]{1,0:T(8,128)}, s32[32,6144]{0,1:T(8,128)}) fusion(s32[6144,32]{1,0:T(8,128)} %copy.25), kind=kLoop, calls=%fused_computation.43 | loop fusion | flops 3932160 | bytes 2752512 | tf_op jit(solution)/shard_map/convert_element_type | solution.py:317
  40.9 2.3 copy.29
  43.3 3.1 copy.31.hi_ref
  46.4 2.0 eq.54
  48.4 3.6 %copy.30 = s32[6144,128]{1,0:T(8,128)} copy(s32[6144,128]{0,1:T(8,128)} %bitcast.34) | data formatting | bytes 6291456 | tf_op jit(solution)/shard_map/eq | solution.py:308
  51.9 3.5 %compare_convert_fusion.low_ref = bf16[6144,128]{1,0:T(8,128)(2,1)} fusion(s32[6144,128]{1,0:T(8,128)} %copy.30, s32[128]{0:T(128)S(1)} %copy-done.6), kind=kLoop, calls=%fused_computation.9 | loop fusion | flops 1572864 | bytes 4719104 | tf_op jit(solution)/shard_map/convert_element_type | solution.py:308
  55.4 5.0 %pad_maximum_fusion.rows_ref = bf16[6144,512]{1,0:T(8,128)(2,1)} fusion(bf16[3072,512]{1,0:T(8,128)(2,1)} %collective-permute-done, bf16[3072,512]{1,0:T(8,128)(2,1)S(1)} %copy-done.2), kind=kLoop, calls=%fused_computation.1 | loop fusion | flops 12582912 | bytes 12582912 | tf_op jit(solution)/shard_map/concatenate | solution.py:285
  60.5 145.2 %all-gather.3.cloned.1.call-done = bf16[16384,512]{1,0:T(8,128)(2,1)} async-done(((bf16[1024,512]{1,0:T(8,128)(2,1)}), bf16[16384,512]{1,0:T(8,128)(2,1)}) %all-gather.3.cloned.1.call-update) | async-done | bytes 16777232 | tf_op jit(solution)/shard_map/all_gather | solution.py:280
  205.7 33.6 %gather_fusion = bf16[6144,512]{1,0:T(8,128)(2,1)} fusion(bf16[16384,512]{1,0:T(8,128)(2,1)} %all-gather.3.cloned.1.call-done, s32[6144]{0:T(1024)S(1)} %broadcast_clamp_fusion), kind=kCustom, calls=%fused_computation | custom fusion | bytes 12607488 | tf_op jit(solution)/shard_map/gather | solution.py:310
  239.4 27.9 %codeword_sums.1 = (bf16[6144,512]{1,0:T(8,128)(2,1)}, f32[256,512]{1,0:T(8,128)}, f32[64,128]{1,0:T(8,128)}) custom-call(bf16[6144,512]{1,0:T(8,128)(2,1)} %pad_maximum_fusion.rows_ref, bf16[6144,512]{1,0:T(8,128)(2,1)} %gather_fusion, s32[32,6144]{1,0:T(8,128)} %copy.31.hi_ref, bf16[6144,128]{1,0:T(8,128)(2,1)} %compare_convert_fusion.low_ref, ...), custom_call_target="tpu_custom_call" | custom-call | flops 12884901888 | bytes 18874368 | tf_op jit(solution)/shard_map/codeword_sums/pallas_call | solution.py:200
  267.2 1.1 select_maximum_fusion.x_ref
  268.4 37.7 %reduce_wide.1 = f32[16,24,512]{2,1,0:T(8,128)S(1)} custom-call(f32[16,24,512]{2,1,0:T(8,128)S(1)} %select_maximum_fusion.x_ref), custom_call_target="tpu_custom_call" | custom-call | tf_op jit(solution)/shard_map/reduce_wide/pallas_call | solution.py:172
  306.2 0.1 add.79
  306.3 0.1 copy.35
  306.4 0.1 add.81
  306.5 0.1 bitcast_add_fusion
  306.6 1.2 fusion.12
  307.8 0.2 copy.36
  308.0 0.5 reshape.221
  308.4 1.9 copy.37
  310.3 1.4 copy.38
  311.8 26.7 %squared_errors.1 = f32[12,1,512]{2,1,0:T(1,128)} custom-call(bf16[6144,512]{1,0:T(8,128)(2,1)} %get-tuple-element.8.resid_ref, bf16[6144,32]{1,0:T(8,128)(2,1)} %get-tuple-element.14.hi_ref, bf16[6144,128]{1,0:T(8,128)(2,1)} %compare_convert_fusion.low_ref, bf16[128,512]{1,0:T(8,128)(2,1)} %fusion.2.spread_ref, bf16[32,2048]{1,0:T(8,128)(2,1)} %reshape.223.widen_ref, ...), custom_call_target="tpu_custom_call" | custom-call | flops 12884901888 | bytes 6291456 | tf_op jit(solution)/shard_map/squared_errors/pallas_call | solution.py:239
  338.5 0.7 fusion.11
  339.2 1.2 collective-permute-done.3
  340.4 0.6 multiply_select_fusion
  341.0 1.5 dynamic-slice_convert_fusion
  342.5 2.3 copy.41
  (31 shorter events, 0.3 us)
Async XLA Ops:
  7.2 1.6 copy-start
  7.2 2.7 copy-start.5
  7.2 3.9 %copy-start.4 = (s32[3072,64]{0,1:T(8,128)S(1)}, s32[3072,64]{0,1:T(8,128)}, u32[]{:S(2)}) copy-start(s32[3072,64]{0,1:T(8,128)} %param.8) | copy-start | bytes 2359300
  7.2 198.5 %all-gather.3.cloned.1.call-start = ((), (), s32[]{:S(2)}) async-start(), calls=%async_computation | async-start | bytes 17825792 | tf_op jit(solution)/shard_map/all_gather | solution.py:280
  9.9 331.1 %all-gather.5.cloned.1.call-start = ((), (), s32[]{:S(2)}) async-start(), calls=%async_computation.1 | async-start | bytes 1572864 | tf_op jit(solution)/shard_map/all_gather | solution.py:322
  9.9 19.9 %collective-permute-start.1 = (s32[3072]{0:T(1024)S(1)}, s32[3072]{0:T(1024)}, u32[]{:S(2)}, u32[]{:S(2)}) collective-permute-start(s32[3072]{0:T(1024)S(1)} %copy-done.5), channel_id=1, source_target_pairs={{0,16},{16,0},{1,17},{17,1},{2,18},{18,2},{3,19},{19,3},{4,20},{20... | collective-permute-start | bytes 36872 | tf_op jit(solution)/shard_map/ppermute | solution.py:289
  12.0 18.6 %collective-permute-start.2 = (s32[3072,32]{0,1:T(8,128)}, s32[3072,32]{0,1:T(8,128)}, u32[]{:S(2)}, u32[]{:S(2)}) collective-permute-start(s32[3072,32]{0,1:T(8,128)} %get-tuple-element.18), channel_id=1, source_target_pairs={{0,16},{16,0},{1,17},{17,1},{2,18},{18,2},{3,19},{19,3},{4,20},{20... | collective-permute-start | bytes 1179656 | tf_op jit(solution)/shard_map/ppermute | solution.py:287
  12.1 6.4 %copy-start.3 = (f32[64,4096]{1,0:T(8,128)S(1)}, f32[64,4096]{1,0:T(8,128)}, u32[]{:S(2)}) copy-start(f32[64,4096]{1,0:T(8,128)} %param.11) | copy-start | bytes 3145732
  18.0 37.4 %collective-permute-start = (bf16[3072,512]{1,0:T(8,128)(2,1)}, bf16[3072,512]{1,0:T(8,128)(2,1)}, u32[]{:S(2)}, u32[]{:S(2)}) collective-permute-start(bf16[3072,512]{1,0:T(8,128)(2,1)} %get-tuple-element.13), channel_id=1, source_target_pairs={{0,16},{16,0},{1,17},{17,1},{2,18},{18,2},{3,19},{19,3},{4,20},{20... | collective-permute-start | bytes 9437192 | tf_op jit(solution)/shard_map/ppermute | solution.py:285
  48.4 3.6 %copy-start.6 = (s32[128]{0:T(128)S(1)}, s32[128]{0:T(128)}, u32[]{:S(2)}) copy-start(s32[128]{0:T(128)} %eq.57) | copy-start | bytes 1540
  51.9 3.5 %copy-start.2 = (bf16[3072,512]{1,0:T(8,128)(2,1)S(1)}, bf16[3072,512]{1,0:T(8,128)(2,1)}, u32[]{:S(2)}) copy-start(bf16[3072,512]{1,0:T(8,128)(2,1)} %get-tuple-element.12) | copy-start | bytes 9437188
  311.7 33.0 %copy-start.1 = (bf16[1024,1024]{1,0:T(8,128)(2,1)S(1)}, bf16[1024,1024]{1,0:T(8,128)(2,1)}, u32[]{:S(2)}) copy-start(bf16[1024,1024]{1,0:T(8,128)(2,1)} %param.10) | copy-start | bytes 6291460
  339.2 1.2 collective-permute-start.3
Sparse Core Ops, SparseCore 0:
  11.4 194.3 all-gather.2
  311.9 10.9 all-gather.4
